TPU v7x, 128 devices: a whole 4x4x4 slice. The times are simulated.
128 devices in a mesh: dp: 16 (over x, z_hi, core), tensor: 8 (over z_lo, y).
Axes of the slice: x: 4, y: 4, z: 4 (z_hi: 2, z_lo: 2; z = z_hi * 2 + z_lo), core: 2. Of those that a mesh axis runs over, the one named last changes fastest.
Arguments:
- residual: bfloat16 [2048, 2880], P('dp'), may hold values from -6 to 6
- attn_gain: bfloat16 [2880], P('dp'), may hold values from 0.5 to 1.5
- query_weight: bfloat16 [2880, 4096], P('dp', 'tensor'), may hold values from -0.109375 to 0.109375
- query_bias: bfloat16 [4096], P('tensor'), may hold values from -0.59765625 to 0.59765625
- key_matrix: bfloat16 [2880, 512], P('dp', 'tensor'), may hold values from -0.109375 to 0.109375
- key_offset_bias: bfloat16 [512], P('tensor'), may hold values from -0.59765625 to 0.59765625
- value_matrix: bfloat16 [2880, 512], P('dp', 'tensor'), may hold values from -0.109375 to 0.109375
- value_offset_bias: bfloat16 [512], P('tensor'), may hold values from -0.59765625 to 0.59765625
- attention_sink_logits: bfloat16 [64], P('tensor'), may hold values from -3 to 3
- out_weight: bfloat16 [2880, 4096], P('dp', 'tensor'), may hold values from -1 to 1
- out_bias: bfloat16 [2880], P('dp'), may hold values from -0.59765625 to 0.59765625
- mlp_gain: bfloat16 [2880], P('dp'), may hold values from 0.5 to 1.5
- router_weight: bfloat16 [2880, 16], P('dp'), may hold values from -0.0546875 to 0.0546875
- router_bias: bfloat16 [16], replicated, may hold values from -0.59765625 to 0.59765625
- gate_weight: bfloat16 [16, 2880, 2880], P('dp', None, 'tensor'), may hold values from -0.109375 to 0.109375
- gate_bias: bfloat16 [16, 2880], P('dp', 'tensor'), may hold values from -0.59765625 to 0.59765625
- up_weight: bfloat16 [16, 2880, 2880], P('dp', None, 'tensor'), may hold values from -0.109375 to 0.109375
- up_bias: bfloat16 [16, 2880], P('dp', 'tensor'), may hold values from -0.59765625 to 0.59765625
- down_weight: bfloat16 [16, 2880, 2880], P('dp', 'tensor'), may hold values from -0.21875 to 0.21875
- down_bias: bfloat16 [16, 2880], P('dp'), may hold values from -0.59765625 to 0.59765625
- routes: int32 [2048, 4], P('dp'), may hold values from 0 to 15, all different within a row; in each aligned block of 128 rows (0 to 127, 128 to 255, ...) at most 64 rows name the same one
- lengths: int32 [3], replicated, may hold values from 1 to 1920, as said below
- cotangent: bfloat16 [2048, 2880], P('dp'), may hold values from -6 to 6
Outputs:
- block_out: float32 [2048, 2880], P('dp')
- grad_input: float32 [2048, 2880], P('dp')
- grad_attn_gain: float32 [2880], P('dp')
- grad_query_weight: float32 [2880, 4096], P('dp', 'tensor')
- grad_query_bias: float32 [4096], P('tensor')
- grad_key_weight: float32 [2880, 512], P('dp', 'tensor')
- grad_key_bias: float32 [512], P('tensor')
- grad_value_weight: float32 [2880, 512], P('dp', 'tensor')
- grad_value_bias: float32 [512], P('tensor')
- grad_attn_sinks: float32 [64], P('tensor')
- grad_out_weight: float32 [2880, 4096], P('dp', 'tensor')
- grad_out_bias: float32 [2880], P('dp')
- grad_mlp_gain: float32 [2880], P('dp')
- grad_router_weight: float32 [2880, 16], P('dp')
- grad_router_bias: float32 [16], replicated
- grad_gate_weight: float32 [16, 2880, 2880], P('dp', None, 'tensor')
- grad_gate_bias: float32 [16, 2880], P('dp', 'tensor')
- grad_up_weight: float32 [16, 2880, 2880], P('dp', None, 'tensor')
- grad_up_bias: float32 [16, 2880], P('dp', 'tensor')
- grad_down_weight: float32 [16, 2880, 2880], P('dp', 'tensor')
- grad_down_bias: float32 [16, 2880], P('dp')
Inputs may be any that keep to these rules, and one draw needn't show every extreme that they name: `lengths`: 3 sequences packed in order; the first and the last together hold 128 tokens, and the middle one holds the other 2048 - 128.
All inputs are finite; a program needn't handle non-finite values.
Results may differ from a plain program's by a relative error of at most 0.024.
Values may be sent and summed in bfloat16 or wider, within the bound.
No kernel may reach another device: no remote copies, remote signals or barrier semaphores. Data moves between devices by JAX's collectives and lax.ppermute only.
A program may use at most 192 MiB of HBM per device.

v0:
```python
import jax
import jax.numpy as jnp
from jax import lax
from jax.sharding import PartitionSpec as P

HEAD_DIM = 64
WINDOW_KEYS = 128


EPSILON = 1e-05
ROPE_BASE = 150000.0
MASKED = -1000000000.0


def from_behind(value, axis, steps):
    count = lax.axis_size(axis)
    leading, last = (max(0, -steps), min(count, count - steps))
    return lax.ppermute(value, axis, [(source, source + steps) for source in range(leading, last)])


def rope_table(position, head_width):
    half_width = head_width // 2
    frequency = ROPE_BASE ** (-2.0 * jnp.arange(half_width, dtype=jnp.float32) / head_width)
    angle_grid = position.astype(jnp.float32)[:, None] * frequency[None, :]
    return (jnp.cos(angle_grid), jnp.sin(angle_grid))


def apply_rotary(heads_in, cosine_values, sine_values):
    half_width = heads_in.shape[-1] // 2
    first_half = heads_in[..., :half_width]
    second_half = heads_in[..., half_width:]
    cos_part = cosine_values[:, None, :]
    sin_part = sine_values[:, None, :]
    return jnp.concatenate(
        [
            first_half * cos_part - second_half * sin_part,
            second_half * cos_part + first_half * sin_part,
        ],
        axis=-1,
    )


def rotate_back(grad_in, cosine_values, sine_values):
    half_width = grad_in.shape[-1] // 2
    first_half = grad_in[..., :half_width]
    second_half = grad_in[..., half_width:]
    cos_part = cosine_values[:, None, :]
    sin_part = sine_values[:, None, :]
    return jnp.concatenate(
        [
            first_half * cos_part + second_half * sin_part,
            second_half * cos_part - first_half * sin_part,
        ],
        axis=-1,
    )


def segments(lengths, token_index):
    seq_ends = jnp.cumsum(lengths)
    seq_starts = seq_ends - lengths
    segment = jnp.sum((token_index[:, None] >= seq_ends[None, :]).astype(jnp.int32), axis=1)
    member = segment[:, None] == jnp.arange(lengths.shape[0], dtype=jnp.int32)[None, :]
    position = token_index - jnp.sum(jnp.where(member, seq_starts[None, :], 0), axis=1)
    return (segment, position)


def norm_forward(values_in):
    scale_row = lax.rsqrt(jnp.mean(values_in * values_in, axis=-1, keepdims=True) + EPSILON)
    return (values_in * scale_row, scale_row)


def norm_back(grad_in, normed, scale_row, gain_row):
    scaled_grad = grad_in * gain_row
    grad_values = scale_row * (
        scaled_grad - normed * jnp.mean(scaled_grad * normed, axis=-1, keepdims=True)
    )
    return (grad_values, jnp.sum(grad_in * normed, axis=0))


def by_expert(arrived, local_experts):
    sources, slot_count, features = arrived.shape
    capacity = slot_count // local_experts
    return (
        arrived.reshape(sources, local_experts, capacity, features)
        .transpose(1, 0, 2, 3)
        .reshape(local_experts, sources * capacity, features)
    )


def by_source(expert_rows, sources):
    local_experts, total_rows, features = expert_rows.shape
    capacity = total_rows // sources
    return (
        expert_rows.reshape(local_experts, sources, capacity, features)
        .transpose(1, 0, 2, 3)
        .reshape(sources, local_experts * capacity, features)
    )


def local(
    residual,
    attn_gain,
    query_weight,
    query_bias,
    key_matrix,
    key_offset_bias,
    value_matrix,
    value_offset_bias,
    attention_sink_logits,
    out_weight,
    out_bias,
    mlp_gain,
    router_weight,
    router_bias,
    gate_weight,
    gate_bias,
    up_weight,
    up_bias,
    down_weight,
    down_bias,
    routes,
    lengths,
    cotangent,
):
    row_count, model_width = residual.shape
    top_k = routes.shape[1]
    experts = router_weight.shape[1]
    local_experts = gate_weight.shape[0]
    dp_count = lax.axis_size("dp")
    head_width = HEAD_DIM
    window = WINDOW_KEYS
    q_heads = attention_sink_logits.shape[0]
    kv_heads = key_offset_bias.shape[0] // head_width
    query_group_count = q_heads // kv_heads
    capacity = 2 * row_count * top_k // experts
    starting_row = lax.axis_index("dp") * row_count
    token_index = starting_row + jnp.arange(row_count, dtype=jnp.int32)
    segment, position = segments(lengths, token_index)
    key_index = starting_row - window + jnp.arange(row_count + window, dtype=jnp.int32)
    key_segment, unused = segments(lengths, key_index)
    offset = token_index[:, None] - key_index[None, :]
    allowed = (
        (segment[:, None] == key_segment[None, :])
        & (offset >= 0)
        & (offset < window)
        & (key_index[None, :] >= 0)
    )
    cosine_values, sine_values = rope_table(position, head_width)
    gathered = (
        lax.all_gather(attn_gain, "dp", axis=0, tiled=True),
        lax.all_gather(query_weight, "dp", axis=0, tiled=True),
        lax.all_gather(key_matrix, "dp", axis=0, tiled=True),
        lax.all_gather(value_matrix, "dp", axis=0, tiled=True),
        lax.all_gather(out_weight, "dp", axis=0, tiled=True),
        lax.all_gather(out_bias, "dp", axis=0, tiled=True),
        lax.all_gather(mlp_gain, "dp", axis=0, tiled=True),
        lax.all_gather(router_weight, "dp", axis=0, tiled=True),
    )
    gain_one, query_full, key_full, value_full, out_full, bias_out, gain_two, router_full = gathered
    gain_one = gain_one.astype(jnp.float32)
    gain_two = gain_two.astype(jnp.float32)
    bias_out = bias_out.astype(jnp.float32)
    inputs = residual.astype(jnp.float32)
    normed_one, scale_one = norm_forward(inputs)
    first_input_half = (normed_one * gain_one).astype(jnp.bfloat16)
    query_lin = jnp.dot(
        first_input_half, query_full, preferred_element_type=jnp.float32
    ) + query_bias.astype(jnp.float32)
    query_rows = apply_rotary(
        query_lin.reshape(row_count, q_heads, head_width), cosine_values, sine_values
    ).astype(jnp.bfloat16)
    key_lin = jnp.dot(
        first_input_half, key_full, preferred_element_type=jnp.float32
    ) + key_offset_bias.astype(jnp.float32)
    keys_own = apply_rotary(
        key_lin.reshape(row_count, kv_heads, head_width), cosine_values, sine_values
    ).astype(jnp.bfloat16)
    value_lin = jnp.dot(
        first_input_half, value_full, preferred_element_type=jnp.float32
    ) + value_offset_bias.astype(jnp.float32)
    values_own = value_lin.astype(jnp.bfloat16).reshape(row_count, kv_heads, head_width)
    rim_keys, rim_values = from_behind((keys_own, values_own), "dp", 1)
    every_key = jnp.concatenate([rim_keys, keys_own], axis=0)
    every_value = jnp.concatenate([rim_values, values_own], axis=0)
    query_group = query_rows.reshape(row_count, kv_heads, query_group_count, head_width)
    scores = 0.125 * jnp.einsum(
        "rkgd,ckd->kgrc", query_group, every_key, preferred_element_type=jnp.float32
    )
    scores = jnp.where(allowed[None, None], scores, MASKED)
    head_sink_logit = attention_sink_logits.astype(jnp.float32).reshape(
        kv_heads, query_group_count
    )[:, :, None]
    peak_score = jnp.maximum(jnp.max(scores, axis=-1), head_sink_logit)
    exp_scores = jnp.exp(scores - peak_score[..., None])
    sink_exp = jnp.exp(head_sink_logit - peak_score)
    denominator = jnp.sum(exp_scores, axis=-1) + sink_exp
    prob_exact = exp_scores / denominator[..., None]
    sink_prob = sink_exp / denominator
    prob_low = prob_exact.astype(jnp.bfloat16)
    heads_out = (
        jnp.einsum("kgrc,ckd->rkgd", prob_low, every_value, preferred_element_type=jnp.float32)
        .astype(jnp.bfloat16)
        .reshape(row_count, q_heads * head_width)
    )
    branch_part = lax.dot_general(
        heads_out, out_full, (((1,), (1,)), ((), ())), preferred_element_type=jnp.float32
    )
    branch_sum = lax.psum(branch_part, "tensor")
    hidden_state = inputs + branch_sum + bias_out
    normed_two, scale_two = norm_forward(hidden_state)
    second_in = (normed_two * gain_two).astype(jnp.bfloat16)
    logits = jnp.dot(
        second_in, router_full, preferred_element_type=jnp.float32
    ) + router_bias.astype(jnp.float32)
    expert_ids = jnp.arange(experts, dtype=jnp.int32)
    picked = routes[:, :, None] == expert_ids[None, None, :]
    chosen = jnp.sum(jnp.where(picked, logits[:, None, :], 0.0), axis=-1)
    gate_probs = jax.nn.softmax(chosen, axis=-1)
    flat_gates = gate_probs.reshape(-1)
    flat_route = routes.reshape(-1)
    onehot = (flat_route[:, None] == expert_ids[None, :]).astype(jnp.int32)
    slot_rank = jnp.sum((jnp.cumsum(onehot, axis=0) - onehot) * onehot, axis=1)
    slot_pos = flat_route * capacity + slot_rank
    source = (
        jnp.full((experts * capacity,), -1, jnp.int32)
        .at[slot_pos]
        .set(jnp.arange(row_count * top_k, dtype=jnp.int32))
    )
    filled = source >= 0
    safe_source = jnp.where(filled, source, 0)
    token_of = safe_source // top_k
    outbound = jnp.where(filled[:, None], second_in[token_of], jnp.zeros((), jnp.bfloat16))
    arrived = lax.all_to_all(
        outbound.reshape(dp_count, local_experts * capacity, model_width),
        "dp",
        split_axis=0,
        concat_axis=0,
        tiled=True,
    )
    expert_rows = by_expert(arrived, local_experts)
    gate_in = (
        jnp.einsum("emd,edf->emf", expert_rows, gate_weight, preferred_element_type=jnp.float32)
        + gate_bias.astype(jnp.float32)[:, None, :]
    )
    up_in = (
        jnp.einsum("emd,edf->emf", expert_rows, up_weight, preferred_element_type=jnp.float32)
        + up_bias.astype(jnp.float32)[:, None, :]
    )
    gate_tanh = jnp.tanh(gate_in / 7.0)
    up_tanh = jnp.tanh(up_in / 7.0)
    gate_c = 7.0 * gate_tanh
    up_c = 7.0 * up_tanh
    sigma = jax.nn.sigmoid(1.702 * gate_c)
    glu_part = gate_c * sigma
    hidden = ((up_c + 1.0) * glu_part).astype(jnp.bfloat16)
    down_out = jnp.einsum("emf,efd->emd", hidden, down_weight, preferred_element_type=jnp.float32)
    bias_on = (lax.axis_index("tensor") == 0).astype(jnp.float32)
    outgoing = by_source(down_out + bias_on * down_bias.astype(jnp.float32)[:, None, :], dp_count)
    owned = jnp.ones((row_count * top_k,), bool)
    returned = (
        lax.all_to_all(outgoing.astype(jnp.bfloat16), "dp", split_axis=0, concat_axis=0, tiled=True)
        .astype(outgoing.dtype)
        .reshape(-1, model_width)
    )
    slot_values = jnp.where(owned[:, None], returned[slot_pos], 0.0).reshape(
        row_count, top_k, model_width
    )
    combined = jnp.sum(gate_probs[:, :, None] * slot_values, axis=1)
    mixture = lax.psum(combined.astype(jnp.bfloat16), "tensor").astype(jnp.float32)
    block_out = hidden_state + mixture
    grad_out = cotangent.astype(jnp.float32)
    gate_grad_part = jnp.sum(slot_values * grad_out[:, None, :], axis=-1)
    slot_grad = jnp.where(
        filled[:, None], flat_gates[safe_source][:, None] * grad_out[token_of], 0.0
    ).astype(jnp.bfloat16)
    grad_arrived = lax.all_to_all(
        slot_grad.reshape(dp_count, local_experts * capacity, model_width),
        "dp",
        split_axis=0,
        concat_axis=0,
        tiled=True,
    )
    down_grad = by_expert(grad_arrived, local_experts)
    act_grad = jnp.einsum(
        "emd,efd->emf", down_grad, down_weight, preferred_element_type=jnp.float32
    )
    grad_down_weight = jnp.einsum(
        "emf,emd->efd", hidden, down_grad, preferred_element_type=jnp.float32
    )
    grad_down_bias = jnp.sum(down_grad, axis=1, dtype=jnp.float32)
    up_c_grad = act_grad * glu_part
    glu_grad = act_grad * (up_c + 1.0)
    gate_c_grad = glu_grad * (sigma + 1.702 * gate_c * sigma * (1.0 - sigma))
    gate_grad = (gate_c_grad * (1.0 - gate_tanh * gate_tanh)).astype(jnp.bfloat16)
    up_grad = (up_c_grad * (1.0 - up_tanh * up_tanh)).astype(jnp.bfloat16)
    grad_gate_weight = jnp.einsum(
        "emd,emf->edf", expert_rows, gate_grad, preferred_element_type=jnp.float32
    )
    grad_gate_bias = jnp.sum(gate_grad, axis=1, dtype=jnp.float32)
    grad_up_weight = jnp.einsum(
        "emd,emf->edf", expert_rows, up_grad, preferred_element_type=jnp.float32
    )
    grad_up_bias = jnp.sum(up_grad, axis=1, dtype=jnp.float32)
    rows_grad = jnp.einsum(
        "emf,edf->emd", gate_grad, gate_weight, preferred_element_type=jnp.float32
    ) + jnp.einsum("emf,edf->emd", up_grad, up_weight, preferred_element_type=jnp.float32)
    grad_outgoing = by_source(rows_grad, dp_count)
    grad_returned = lax.all_to_all(
        grad_outgoing, "dp", split_axis=0, concat_axis=0, tiled=True
    ).reshape(-1, model_width)
    second_part = jnp.sum(
        jnp.where(owned[:, None], grad_returned[slot_pos], 0.0).reshape(
            row_count, top_k, model_width
        ),
        axis=1,
    )
    second_sum, gate_grads = lax.psum((second_part, gate_grad_part), "tensor")
    chosen_grad = gate_probs * (
        gate_grads - jnp.sum(gate_probs * gate_grads, axis=-1, keepdims=True)
    )
    logit_grad = jnp.sum(jnp.where(picked, chosen_grad[:, :, None], 0.0), axis=1)
    grad_router_weight = jnp.einsum(
        "rd,re->de", second_in, logit_grad, preferred_element_type=jnp.float32
    )
    grad_router_bias = jnp.sum(logit_grad, axis=0)
    second_grad = second_sum + jnp.einsum(
        "re,de->rd", logit_grad, router_full, preferred_element_type=jnp.float32
    )
    state_norm_grad, grad_mlp_gain = norm_back(second_grad, normed_two, scale_two, gain_two)
    state_grad = grad_out + state_norm_grad
    grad_out_bias = jnp.sum(state_grad, axis=0)
    state_low = state_grad.astype(jnp.bfloat16)
    heads_grad = jnp.dot(state_low, out_full, preferred_element_type=jnp.float32).astype(
        jnp.bfloat16
    )
    grad_out_weight = jnp.einsum(
        "rd,rh->dh", state_low, heads_out, preferred_element_type=jnp.float32
    )
    heads_group = heads_grad.reshape(row_count, kv_heads, query_group_count, head_width)
    prob_grad = jnp.einsum(
        "rkgd,ckd->kgrc", heads_group, every_value, preferred_element_type=jnp.float32
    )
    row_delta = jnp.sum(prob_exact * prob_grad, axis=-1)
    score_grad = (prob_exact * (prob_grad - row_delta[..., None])).astype(jnp.bfloat16)
    grad_sinks = -jnp.sum(sink_prob * row_delta, axis=-1).reshape(q_heads)
    query_grad = 0.125 * jnp.einsum(
        "kgrc,ckd->rkgd", score_grad, every_key, preferred_element_type=jnp.float32
    ).reshape(row_count, q_heads, head_width)
    keys_grad = 0.125 * jnp.einsum(
        "kgrc,rkgd->ckd", score_grad, query_group, preferred_element_type=jnp.float32
    )
    values_grad = jnp.einsum(
        "kgrc,rkgd->ckd", prob_low, heads_group, preferred_element_type=jnp.float32
    )
    rim_key_grad, rim_value_grad = (
        from_behind(keys_grad[:window].astype(jnp.bfloat16), "dp", -1).astype(jnp.float32),
        from_behind(values_grad[:window].astype(jnp.bfloat16), "dp", -1).astype(jnp.float32),
    )
    key_grad = keys_grad[window:].at[row_count - window :].add(rim_key_grad)
    value_grad = values_grad[window:].at[row_count - window :].add(rim_value_grad)
    query_lin_grad = (
        rotate_back(query_grad, cosine_values, sine_values)
        .reshape(row_count, -1)
        .astype(jnp.bfloat16)
    )
    key_lin_grad = (
        rotate_back(key_grad, cosine_values, sine_values)
        .reshape(row_count, -1)
        .astype(jnp.bfloat16)
    )
    value_lin_grad = value_grad.reshape(row_count, -1).astype(jnp.bfloat16)
    grad_query_weight = jnp.einsum(
        "rd,rh->dh", first_input_half, query_lin_grad, preferred_element_type=jnp.float32
    )
    grad_key_weight = jnp.einsum(
        "rd,rh->dh", first_input_half, key_lin_grad, preferred_element_type=jnp.float32
    )
    grad_value_weight = jnp.einsum(
        "rd,rh->dh", first_input_half, value_lin_grad, preferred_element_type=jnp.float32
    )
    grad_query_bias = jnp.sum(query_lin_grad, axis=0, dtype=jnp.float32)
    grad_key_bias = jnp.sum(key_lin_grad, axis=0, dtype=jnp.float32)
    grad_value_bias = jnp.sum(value_lin_grad, axis=0, dtype=jnp.float32)
    first_part = lax.dot_general(
        query_lin_grad, query_full, (((1,), (1,)), ((), ())), preferred_element_type=jnp.float32
    )
    first_part = first_part + lax.dot_general(
        key_lin_grad, key_full, (((1,), (1,)), ((), ())), preferred_element_type=jnp.float32
    )
    first_part = first_part + lax.dot_general(
        value_lin_grad, value_full, (((1,), (1,)), ((), ())), preferred_element_type=jnp.float32
    )
    first_grad = lax.psum(first_part.astype(jnp.bfloat16), "tensor").astype(jnp.float32)
    input_norm_grad, grad_attn_gain = norm_back(first_grad, normed_one, scale_one, gain_one)
    grad_input = state_grad + input_norm_grad
    dense_grads = (
        lax.psum_scatter(
            grad_attn_gain.astype(jnp.bfloat16), "dp", scatter_dimension=0, tiled=True
        ).astype(jnp.float32),
        lax.psum_scatter(
            grad_query_weight.astype(jnp.bfloat16), "dp", scatter_dimension=0, tiled=True
        ).astype(jnp.float32),
        lax.psum_scatter(
            grad_key_weight.astype(jnp.bfloat16), "dp", scatter_dimension=0, tiled=True
        ).astype(jnp.float32),
        lax.psum_scatter(
            grad_value_weight.astype(jnp.bfloat16), "dp", scatter_dimension=0, tiled=True
        ).astype(jnp.float32),
        lax.psum_scatter(
            grad_out_weight.astype(jnp.bfloat16), "dp", scatter_dimension=0, tiled=True
        ).astype(jnp.float32),
        lax.psum_scatter(
            grad_out_bias.astype(jnp.bfloat16), "dp", scatter_dimension=0, tiled=True
        ).astype(jnp.float32),
        lax.psum_scatter(
            grad_mlp_gain.astype(jnp.bfloat16), "dp", scatter_dimension=0, tiled=True
        ).astype(jnp.float32),
        lax.psum_scatter(
            grad_router_weight.astype(jnp.bfloat16), "dp", scatter_dimension=0, tiled=True
        ).astype(jnp.float32),
    )
    small_grads = lax.psum(
        (grad_query_bias, grad_key_bias, grad_value_bias, grad_sinks, grad_router_bias), "dp"
    )
    return (
        block_out,
        grad_input,
        dense_grads[0],
        dense_grads[1],
        small_grads[0],
        dense_grads[2],
        small_grads[1],
        dense_grads[3],
        small_grads[2],
        small_grads[3],
        dense_grads[4],
        dense_grads[5],
        dense_grads[6],
        dense_grads[7],
        small_grads[4],
        grad_gate_weight,
        grad_gate_bias,
        grad_up_weight,
        grad_up_bias,
        grad_down_weight,
        grad_down_bias,
    )


def solution(mesh):
    return jax.shard_map(
        local,
        mesh=mesh,
        in_specs=(
            P("dp", None),
            P("dp"),
            P("dp", "tensor"),
            P("tensor"),
            P("dp", "tensor"),
            P("tensor"),
            P("dp", "tensor"),
            P("tensor"),
            P("tensor"),
            P("dp", "tensor"),
            P("dp"),
            P("dp"),
            P("dp", None),
            P(),
            P("dp", None, "tensor"),
            P("dp", "tensor"),
            P("dp", None, "tensor"),
            P("dp", "tensor"),
            P("dp", "tensor", None),
            P("dp", None),
            P("dp", None),
            P(),
            P("dp", None),
        ),
        out_specs=(
            P("dp", None),
            P("dp", None),
            P("dp"),
            P("dp", "tensor"),
            P("tensor"),
            P("dp", "tensor"),
            P("tensor"),
            P("dp", "tensor"),
            P("tensor"),
            P("tensor"),
            P("dp", "tensor"),
            P("dp"),
            P("dp"),
            P("dp", None),
            P(),
            P("dp", None, "tensor"),
            P("dp", "tensor"),
            P("dp", None, "tensor"),
            P("dp", "tensor"),
            P("dp", "tensor", None),
            P("dp", None),
        ),
        check_vma=False,
    )
```

profile of v0, /device:TPU:0, one launch (start us, length us, event | category | flops | bytes accessed | tf_op | source)
XLA Modules:
  0.0 1327.4 jit_solution(13423958197505869829)
XLA Ops:
  14.0 70.9 %all-reduce.15 = (bf16[2880]{0:T(1024)(128)(2,1)S(1)}, bf16[2880]{0:T(1024)(128)(2,1)S(1)}, bf16[2880]{0:T(1024)(128)(2,1)S(1)}) all-reduce(bf16[2880]{0:T(1024)(128)(2,1)S(1)} %dynamic-update-slice.4, bf16[2880]{0:T(1024)(128)(2,1)S(1)} %dynamic-update-slice.5, ...), channel_id=1, replica_groups=mesh['dp'=16,'tensor'=8] {'dp'}, use_global_device_ids=true, to_apply=%add | all-reduce | flops 8640 | bytes 34560
  84.9 21.9 %all-gather.1 = bf16[16,180,64]{1,2,0:T(8,128)(2,1)S(1)} all-gather(bf16[1,180,64]{1,2,0:T(8,128)(2,1)} %bitcast.212), channel_id=1, replica_groups=mesh['dp'=16,'tensor'=8] {'dp'}, dimensions={0}, use_global_device_ids=true | all-gather | bytes 391680 | tf_op jit(solution)/shard_map/all_gather | solution.py:152
  113.5 24.0 %all-gather = bf16[16,180,64]{1,2,0:T(8,128)(2,1)S(1)} all-gather(bf16[1,180,64]{1,2,0:T(8,128)(2,1)S(1)} %bitcast.213), channel_id=1, replica_groups=mesh['dp'=16,'tensor'=8] {'dp'}, dimensions={0}, use_global_device_ids=true | all-gather | bytes 391680 | tf_op jit(solution)/shard_map/all_gather | solution.py:153
  169.0 72.0 %all-reduce.24.cloned.1.call-done = f32[128,2880]{0,1:T(8,128)} async-done(((f32[128,2880]{0,1:T(8,128)}), f32[128,2880]{0,1:T(8,128)}) %all-reduce.24.cloned.1.call-update) | async-done | bytes 1474576 | tf_op jit(solution)/shard_map/psum | solution.py:208
  266.1 87.5 %all-to-all-done = bf16[16,64,2880]{2,1,0:T(8,128)(2,1)} async-done(((bf16[16,64,2880]{2,1,0:T(8,128)(2,1)}), bf16[16,64,2880]{2,1,0:T(8,128)(2,1)}, u32[]{:S(2)}, u32[]{:S(2)}) %all-to-all-start) | async-done | bytes 5898272 | tf_op jit(solution)/shard_map/all_to_all | solution.py:233
  372.2 8.5 copy.112
  380.7 12.3 all-to-all-start.1
  393.0 108.4 %all-gather.4 = bf16[16,180,16]{1,2,0:T(8,128)(2,1)S(1)} all-gather(bf16[1,180,16]{1,2,0:T(8,128)(2,1)S(1)} %bitcast.214), channel_id=1, replica_groups=mesh['dp'=16,'tensor'=8] {'dp'}, dimensions={0}, use_global_device_ids=true | all-gather | bytes 97920 | tf_op jit(solution)/shard_map/all_gather | solution.py:157
  503.1 12.8 gather_fusion.3
  520.9 7.9 mul.446
  529.1 7.9 bitcast_convert_fusion
  536.9 11.4 gather_fusion.1
  553.6 17.2 %psum.73 = f32[128,4]{0,1:T(4,128)S(1)} all-reduce(f32[128,4]{0,1:T(4,128)S(1)} %copy.119), channel_id=1, replica_groups=mesh['dp'=16,'tensor'=8] {'tensor'}, use_global_device_ids=true, to_apply=%region_21.22 | all-reduce | flops 512 | bytes 4096 | tf_op jit(solution)/shard_map/psum | solution.py:317
  577.9 9.7 select_convert_fusion
  587.6 75.4 %all_to_all.20 = bf16[16,64,2880]{2,1,0:T(8,128)(2,1)S(1)} all-to-all(bf16[16,64,2880]{2,1,0:T(8,128)(2,1)} %select_convert_fusion), channel_id=1, replica_groups=mesh['dp'=16,'tensor'=8] {'dp'}, dimensions={0} | all-to-all | bytes 11796480 | tf_op jit(solution)/shard_map/all_to_all | solution.py:276
  676.3 12.3 copy.116
  719.2 166.8 %all-to-all-done.3 = f32[16,64,2880]{2,1,0:T(8,128)} async-done(((f32[16,64,2880]{2,1,0:T(8,128)}), f32[16,64,2880]{2,1,0:T(8,128)}, u32[]{:S(2)}, u32[]{:S(2)}) %all-to-all-start.3) | async-done | bytes 11796512 | tf_op jit(solution)/shard_map/all_to_all | solution.py:308
  886.0 11.4 gather_fusion.4
  933.3 59.0 %all-reduce.26.cloned.1.call-done = f32[128,2880]{0,1:T(8,128)} async-done(((f32[128,2880]{0,1:T(8,128)}), f32[128,2880]{0,1:T(8,128)}) %all-reduce.26.cloned.1.call-update) | async-done | bytes 1474576 | tf_op jit(solution)/shard_map/psum | solution.py:317
  1016.5 77.8 %fusion.96 = (bf16[184,512]{1,0:T(8,128)(2,1)S(1)}, bf16[184,512]{1,0:T(8,128)(2,1)S(1)}) fusion(bf16[2880,512]{1,0:T(8,128)(2,1)} %convolution_convert_fusion.1, bf16[2880,512]{1,0:T(8,128)(2,1)} %convolution_convert_fusion), kind=kCustom, calls=%all-reduce-scatter.2 | all-reduce-scatter fusion | flops 3014657 | bytes 6275584
  1106.4 33.8 %all-reduce.13 = (f32[512]{0:T(512)}, f32[64]{0:T(128)}, f32[64]{0:T(128)}, f32[8]{0:T(128)}, f32[16]{0:T(128)}) all-reduce(f32[512]{0:T(512)S(1)} %reduce_sum.285, f32[64]{0:T(128)S(1)} %convert_reduce_fusion.5, f32[64]{0:T(128)S(1)} %get-tuple-element.91, f32[8]{0:T(128)S(1)} %neg.8, ...), channel_id=1, replica_groups=mesh['dp'=16,'tensor'=8] {'dp'}, use_global_device_ids=true, to_apply=%region_32.33 | all-reduce | flops 664 | bytes 5312 | tf_op jit(solution)/shard_map/psum | solution.py:422
  1142.3 24.9 %all-reduce.28.cloned.1.call-done = (bf16[2880,64]{0,1:T(8,128)(2,1)}, bf16[2880,64]{0,1:T(8,128)(2,1)}, bf16[2880,16]{0,1:T(8,128)(2,1)}) async-done(((bf16[2880,64]{0,1:T(8,128)(2,1)}, bf16[2880,64]{0,1:T(8,128)(2,1)}, bf16[2880,16]{0,1:T(8,128)(2,1)}), (bf16[2880,64]{0,1:T(8,128)(2,1)}, bf16[2880,64]{0,1:T(8,128)(2,1)}, bf16[2880,16]{0,1:T(8,128)(2,1)})) %all-reduce.28.cloned.1.call-update) | async-done | bytes 829456
  1170.2 77.0 %all-reduce.30.cloned.1.call-done = (bf16[128,2880]{0,1:T(8,128)(2,1)}, bf16[128,2880]{0,1:T(8,128)(2,1)}) async-done(((bf16[128,2880]{0,1:T(8,128)(2,1)}, bf16[128,2880]{0,1:T(8,128)(2,1)}), (bf16[128,2880]{0,1:T(8,128)(2,1)}, bf16[128,2880]{0,1:T(8,128)(2,1)})) %all-reduce.30.cloned.1.call-update) | async-done | bytes 1474576 | tf_op jit(solution)/shard_map/psum | solution.py:269
  1249.2 65.1 %all-reduce.14 = (bf16[2880]{0:T(1024)(128)(2,1)S(1)}, bf16[2880]{0:T(1024)(128)(2,1)S(1)}, bf16[2880]{0:T(1024)(128)(2,1)S(1)}) all-reduce(bf16[2880]{0:T(1024)(128)(2,1)S(1)} %get-tuple-element.63, bf16[2880]{0:T(1024)(128)(2,1)S(1)} %get-tuple-element.95, ...), channel_id=2, replica_groups=mesh['dp'=16,'tensor'=8] {'dp'}, use_global_device_ids=true, to_apply=%region_29.30.clone | all-reduce | flops 8640 | bytes 34560
  (340 shorter events, 234.0 us)
Async XLA Ops:
  7.2 359.7 %copy-start = (bf16[1,360,2880]{2,1,0:T(8,128)(2,1)S(1)}, bf16[1,360,2880]{2,1,0:T(8,128)(2,1)}, u32[]{:S(2)}) copy-start(bf16[1,360,2880]{2,1,0:T(8,128)(2,1)} %param.49) | copy-start | bytes 6220804
  7.2 137.6 %all-gather.8.cloned.1.call-start = ((), (), s32[]{:S(2)}) async-start(), calls=%async_computation.6 | async-start | bytes 3203072 | tf_op jit(solution)/shard_map/all_gather | solution.py:151
  7.3 101.4 %copy-start.69 = (s32[3]{0:T(128)S(1)}, s32[3]{0:T(128)}, u32[]{:S(2)}) copy-start(s32[3]{0:T(128)} %param.52) | copy-start | bytes 40
  7.3 101.7 %copy-start.6 = (bf16[128,2880]{0,1:T(8,128)(2,1)S(1)}, bf16[128,2880]{0,1:T(8,128)(2,1)}, u32[]{:S(2)}) copy-start(bf16[128,2880]{0,1:T(8,128)(2,1)} %param.31) | copy-start | bytes 2211844
  7.9 146.7 %all-gather.10.cloned.1.call-start = ((), (), s32[]{:S(2)}) async-start(), calls=%async_computation.7 | async-start | bytes 3203072 | tf_op jit(solution)/shard_map/all_gather | solution.py:154
  8.7 232.3 %all-reduce.24.cloned.1.call-start = ((), (), s32[]{:S(2)}) async-start(), calls=%async_computation.4 | async-start | bytes 2949120 | tf_op jit(solution)/shard_map/psum | solution.py:208
  111.2 41.2 %collective-permute-start.1 = (bf16[128,1,64]{0,2,1:T(8,128)(2,1)S(1)}, bf16[128,1,64]{0,2,1:T(8,128)(2,1)S(1)}, u32[]{:S(2)}, u32[]{:S(2)}) collective-permute-start(bf16[128,1,64]{0,2,1:T(8,128)(2,1)S(1)} %pad_maximum_fusion.3), channel_id=1, source_target_pairs={{0,8},{8,16},{16,24},{24,32},{32,40},{40,48},{48,56},{56,64},{64,7... | collective-permute-start | bytes 49160 | tf_op jit(solution)/shard_map/ppermute | solution.py:18
  141.5 17.5 %collective-permute-start = (bf16[128,1,64]{0,2,1:T(8,128)(2,1)}, bf16[128,1,64]{0,2,1:T(8,128)(2,1)}, u32[]{:S(2)}, u32[]{:S(2)}) collective-permute-start(bf16[128,1,64]{0,2,1:T(8,128)(2,1)} %fusion.36), channel_id=1, source_target_pairs={{0,8},{8,16},{16,24},{24,32},{32,40},{40,48},{48,56},{56,64},{64,7... | collective-permute-start | bytes 49160 | tf_op jit(solution)/shard_map/ppermute | solution.py:18
  164.5 78.4 %copy-start.32 = (f32[2880]{0:T(1024)}, f32[2880]{0:T(1024)S(1)}, u32[]{:S(2)}) copy-start(f32[2880]{0:T(1024)S(1)} %convert_element_type.249) | copy-start | bytes 34564
  259.2 94.5 %all-to-all-start = ((bf16[16,64,2880]{2,1,0:T(8,128)(2,1)}), bf16[16,64,2880]{2,1,0:T(8,128)(2,1)}, u32[]{:S(2)}, u32[]{:S(2)}) async-start(bf16[16,64,2880]{2,1,0:T(8,128)(2,1)} %broadcast_select_fusion), calls=%async_computation | async-start | bytes 12058624 | tf_op jit(solution)/shard_map/all_to_all | solution.py:233
  380.7 121.0 %copy-start.13 = (bf16[128,2880]{0,1:T(8,128)(2,1)S(1)}, bf16[128,2880]{0,1:T(8,128)(2,1)}, u32[]{:S(2)}) copy-start(bf16[128,2880]{0,1:T(8,128)(2,1)} %param.53) | copy-start | bytes 2211844
  380.7 148.4 %all-to-all-start.1 = ((bf16[16,64,2880]{2,1,0:T(8,128)(2,1)}), bf16[16,64,2880]{2,1,0:T(8,128)(2,1)}, u32[]{:S(2)}, u32[]{:S(2)}) async-start(bf16[16,64,2880]{2,1,0:T(8,128)(2,1)} %bitcast.201), calls=%async_computation.1 | async-start | bytes 12058624 | tf_op jit(solution)/shard_map/all_to_all | solution.py:261
  587.6 75.4 %copy-start.77 = (f32[1024,360]{0,1:T(8,128)S(1)}, f32[1024,360]{0,1:T(8,128)}, u32[]{:S(2)}) copy-start(f32[1024,360]{0,1:T(8,128)} %get-tuple-element.121) | copy-start | bytes 4423684
  688.6 197.4 %all-to-all-start.3 = ((f32[16,64,2880]{2,1,0:T(8,128)}), f32[16,64,2880]{2,1,0:T(8,128)}, u32[]{:S(2)}, u32[]{:S(2)}) async-start(f32[16,64,2880]{2,1,0:T(8,128)} %bitcast.197), calls=%async_computation.3 | async-start | bytes 24117248 | tf_op jit(solution)/shard_map/all_to_all | solution.py:308
  693.5 298.8 %all-reduce.26.cloned.1.call-start = ((), (), s32[]{:S(2)}) async-start(), calls=%async_computation.5 | async-start | bytes 2949120 | tf_op jit(solution)/shard_map/psum | solution.py:317
  912.9 254.3 %all-reduce.28.cloned.1.call-start = ((), (), s32[]{:S(2)}) async-start(), calls=%async_computation.8 | async-start | bytes 1695744
  1000.6 8.2 collective-permute-start.3
  1004.5 5.8 collective-permute-start.2
  1011.8 235.4 %all-reduce.30.cloned.1.call-start = ((), (), s32[]{:S(2)}) async-start(), calls=%async_computation.9 | async-start | bytes 2949120 | tf_op jit(solution)/shard_map/psum | solution.py:269
  1016.4 89.5 %copy-start.45 = (f32[8,128]{1,0:T(8,128)S(1)}, f32[8,128]{1,0:T(8,128)}, u32[]{:S(2)}) copy-start(f32[8,128]{1,0:T(8,128)} %copy-done.44) | copy-start | bytes 12292
  1016.4 89.5 %copy-start.47 = (f32[8,128]{1,0:T(8,128)S(1)}, f32[8,128]{1,0:T(8,128)}, u32[]{:S(2)}) copy-start(f32[8,128]{1,0:T(8,128)} %copy-done.46) | copy-start | bytes 12292
  1016.5 89.5 %copy-start.63 = (f32[8]{0:T(128)S(1)}, f32[8]{0:T(128)}, u32[]{:S(2)}) copy-start(f32[8]{0:T(128)} %copy-done.62) | copy-start | bytes 100
  1094.4 45.8 %collective-permute-start.5 = (bf16[60,512]{1,0:T(8,128)(2,1)S(1)}, bf16[60,512]{1,0:T(8,128)(2,1)S(1)}, u32[]{:S(2)}, u32[]{:S(2)}) collective-permute-start(bf16[60,512]{1,0:T(8,128)(2,1)S(1)} %slice.120), channel_id=1, source_target_pairs={{0,8},{8,16},{16,24},{24,32},{32,40},{40,48},{48,56},{56,64},{64,7... | collective-permute-start | bytes 184328
  1100.0 40.4 %collective-permute-start.4 = (bf16[60,512]{1,0:T(8,128)(2,1)S(1)}, bf16[60,512]{1,0:T(8,128)(2,1)S(1)}, u32[]{:S(2)}, u32[]{:S(2)}) collective-permute-start(bf16[60,512]{1,0:T(8,128)(2,1)S(1)} %slice.119), channel_id=1, source_target_pairs={{0,8},{8,16},{16,24},{24,32},{32,40},{40,48},{48,56},{56,64},{64,7... | collective-permute-start | bytes 184328
  (69 other events, 832.3 us)
Sparse Core Ops, SparseCore 0:
  10.4 54.5 all-gather.7
  67.4 50.7 all-gather.9
  163.6 77.3 all-reduce.23
  913.1 79.1 all-reduce.25
  1011.9 155.3 all-reduce.27
  1169.9 77.2 all-reduce.29
where the time goes:
time: 1340 us; the launch traced here: 1330 us
  blocking collectives  494 us (37%)
  waiting for transfers between devices  489 us (36%)
  local copies, waits for them, and re-layouts  132 us (10%)
  matrix products  82.9 us (6%)
  other arithmetic  67.2 us (5%)
  starting transfers between devices  44.2 us (3%)
  between operations  17.9 us (1%)
    unnamed x3, blocking collectives  214 us
    all_to_all x1, waiting for transfers between devices, local(): lax.all_to_all(grad_outgoing, 'dp', split_axis=0, concat_axis=0, tiled=True)  167 us
    all_gather x1, blocking collectives, local(): lax.all_gather(router_weight, 'dp', axis=0, tiled=True)  108 us
    all_to_all x1, waiting for transfers between devices, local(): lax.all_to_all(outbound.reshape(dp_count, local_experts * capacity, model...  87.5 us
    psum x1, waiting for transfers between devices, local(): lax.psum(combined.astype(jnp.bfloat16), 'tensor').astype(jnp.float32)  77 us
    all_to_all x1, blocking collectives, local(): lax.all_to_all(slot_grad.reshape(dp_count, local_experts * capacity, mode...  75.4 us
    psum x1, waiting for transfers between devices, local(): branch_sum = lax.psum(branch_part, 'tensor')  72 us
    psum x1, waiting for transfers between devices, local(): second_sum, gate_grads = lax.psum((second_part, gate_grad_part), 'tensor')  59 us
  transfers between devices with their start and end apart: 15, of which 6 were waited for; matrix products, arithmetic and copies ran while one was open for 15% of the time, Pallas kernels for 0%

commit v1 on v0

v1 whole, which is shorter than its diff:
```python
import jax
import jax.numpy as jnp
from jax import lax
from jax.sharding import PartitionSpec as P

HEAD_DIM = 64
WINDOW_KEYS = 128
EPSILON = 1e-05
ROPE_BASE = 150000.0
MASKED = -1000000000.0
BF = jnp.bfloat16
F32 = jnp.float32


def rope_table(position, head_width):
    half_width = head_width // 2
    frequency = ROPE_BASE ** (-2.0 * jnp.arange(half_width, dtype=F32) / head_width)
    angle_grid = position.astype(F32)[:, None] * frequency[None, :]
    return (jnp.cos(angle_grid), jnp.sin(angle_grid))


def rotate(heads_in, cos, sin):
    half = heads_in.shape[-1] // 2
    a, b = heads_in[..., :half], heads_in[..., half:]
    c, s = cos[:, None, :], sin[:, None, :]
    return jnp.concatenate([a * c - b * s, b * c + a * s], axis=-1)


def segments(lengths, token_index):
    seq_ends = jnp.cumsum(lengths)
    seq_starts = seq_ends - lengths
    segment = jnp.sum((token_index[:, None] >= seq_ends[None, :]).astype(jnp.int32), axis=1)
    member = segment[:, None] == jnp.arange(lengths.shape[0], dtype=jnp.int32)[None, :]
    position = token_index - jnp.sum(jnp.where(member, seq_starts[None, :], 0), axis=1)
    return (segment, position)


def exchange(value, axis):
    return lax.all_to_all(value, axis, split_axis=0, concat_axis=0, tiled=True)


def spread(value, axis):
    count = lax.axis_size(axis)
    return exchange(jnp.broadcast_to(value[None], (count,) + value.shape), axis)


def dot(a, b, dims=((1,), (0,))):
    return lax.dot_general(a, b, (dims, ((), ())), preferred_element_type=F32)


def high_low(value):
    high = value.astype(BF)
    return high, (value - high.astype(F32)).astype(BF)


def local(
    residual,
    attn_gain,
    query_weight,
    query_bias,
    key_matrix,
    key_offset_bias,
    value_matrix,
    value_offset_bias,
    attention_sink_logits,
    out_weight,
    out_bias,
    mlp_gain,
    router_weight,
    router_bias,
    gate_weight,
    gate_bias,
    up_weight,
    up_bias,
    down_weight,
    down_bias,
    routes,
    lengths,
    cotangent,
):
    rows, width = residual.shape
    experts = router_weight.shape[1]
    dp = lax.axis_size("dp")
    tn = lax.axis_size("tensor")
    me_dp = lax.axis_index("dp")
    me_t = lax.axis_index("tensor")
    hd = HEAD_DIM
    window = WINDOW_KEYS
    q_heads = attention_sink_logits.shape[0]
    cap = 2 * rows * routes.shape[1] // experts
    chunk = width // dp
    chunk_pad = 192
    cols = 384
    wide = tn * cols
    spare = width - (tn - 1) * cols
    slots = experts * cap

    def padded(a):
        return jnp.pad(a, ((0, 0), (0, wide - width)))

    def my_cols(a):
        return lax.dynamic_slice_in_dim(a, me_t * cols, cols, 1)

    def by_chunk(a):
        a = jnp.pad(a.reshape(rows, dp, chunk), ((0, 0), (0, 0), (0, chunk_pad - chunk)))
        a = a.transpose(1, 0, 2)
        return jnp.concatenate([a[:, : rows // 2], a[:, rows // 2 :]], axis=2)

    def of_chunk(a):
        first = a[:, :, :chunk].reshape(dp * rows // 2, chunk)
        second = a[:, :, chunk_pad : chunk_pad + chunk].reshape(dp * rows // 2, chunk)
        return first, second

    expert_ids = jnp.arange(experts, dtype=jnp.int32)
    member = jnp.any(routes[:, :, None] == expert_ids[None, None, :], axis=1)
    member_f = member.astype(F32)
    below = (jnp.arange(rows)[:, None] > jnp.arange(rows)[None, :]).astype(BF)
    rank = dot(below, member.astype(BF)).astype(jnp.int32)
    place = (
        (rank.T[:, None, :] == jnp.arange(cap, dtype=jnp.int32)[None, :, None])
        & member.T[:, None, :]
    ).astype(BF)
    place2 = place.reshape(slots, rows)

    extras = jnp.concatenate(
        [attn_gain[None], mlp_gain[None], out_bias[None], router_weight.T, jnp.zeros((2, chunk), BF)]
    ).reshape(7, 3, chunk)
    extras = jnp.pad(extras, ((0, 0), (0, 0), (0, chunk_pad - chunk))).reshape(7, 3 * chunk_pad)
    own_qkv = jnp.concatenate([query_weight, key_matrix, value_matrix], axis=1)
    qkv_cols = own_qkv.shape[1]
    extras = jnp.pad(extras, ((0, chunk_pad - chunk - 7), (0, qkv_cols - 3 * chunk_pad)))
    qkv_all = lax.all_gather(jnp.concatenate([own_qkv, extras], axis=0), "dp")
    out_all = lax.all_gather(
        jnp.pad(out_weight, ((0, chunk_pad - chunk), (0, 0))), "dp"
    )
    small = (
        qkv_all[:, chunk : chunk + 7, : 3 * chunk_pad]
        .reshape(dp, 21, chunk_pad)[:, :, :chunk]
        .transpose(1, 0, 2)
        .reshape(21, width)
    )
    gain_one = small[0].astype(F32)
    gain_two = small[1].astype(F32)
    bias_out = small[2].astype(F32)
    router_t = small[3 : 3 + experts]

    inputs = residual.astype(F32)
    scale_one = lax.rsqrt(jnp.mean(inputs * inputs, axis=-1, keepdims=True) + EPSILON)
    normed_one = inputs * scale_one
    grad_ext = jnp.concatenate(
        [cotangent, member.astype(BF), jnp.zeros((rows, wide - width - experts), BF)], axis=1
    )
    grad_slots = dot(place2, my_cols(grad_ext)).astype(BF).reshape(experts, cap, cols)
    first_got = exchange(
        jnp.concatenate([grad_slots, by_chunk(normed_one.astype(BF))], axis=1), "dp"
    )
    grad_rows = lax.all_gather(first_got[:, :cap].reshape(slots, cols), "tensor")
    grad_rows = grad_rows.transpose(1, 0, 2).reshape(slots, wide)
    first_chunk = tuple(
        (half.astype(F32) * attn_gain.astype(F32)[None]).astype(BF)
        for half in of_chunk(first_got[:, cap:])
    )

    starting_row = me_dp * rows
    token_index = starting_row + jnp.arange(rows, dtype=jnp.int32)
    segment, position = segments(lengths, token_index)
    key_index = starting_row - window + jnp.arange(rows + window, dtype=jnp.int32)
    key_segment, unused = segments(lengths, key_index)
    offset = token_index[:, None] - key_index[None, :]
    allowed = (
        (segment[:, None] == key_segment[None, :])
        & (offset >= 0)
        & (offset < window)
        & (key_index[None, :] >= 0)
    )
    cos, sin = rope_table(position, hd)
    normed_pad = jnp.pad(
        normed_one.reshape(rows, dp, chunk), ((0, 0), (0, 0), (0, chunk_pad - chunk))
    )
    gain_pad = qkv_all[:, chunk, :chunk_pad].astype(F32)
    first_in = (normed_pad * gain_pad[None]).astype(BF).reshape(rows, dp * chunk_pad)
    qkv_bias = jnp.concatenate([query_bias, key_offset_bias, value_offset_bias]).astype(F32)
    lin = dot(first_in, qkv_all.reshape(dp * chunk_pad, qkv_cols)) + qkv_bias
    q_cols = q_heads * hd
    query = rotate(lin[:, :q_cols].reshape(rows, q_heads, hd), cos, sin).astype(BF)
    key_own = rotate(lin[:, None, q_cols : q_cols + hd], cos, sin).astype(BF)[:, 0]
    value_own = lin[:, q_cols + hd :].astype(BF)
    own_kv = jnp.concatenate([key_own, value_own], axis=1)
    rim_kv = lax.ppermute(own_kv, "dp", [(i, i + 1) for i in range(dp - 1)])
    keys = jnp.concatenate([rim_kv[:, :hd], key_own], axis=0)
    values = jnp.concatenate([rim_kv[:, hd:], value_own], axis=0)
    scores = 0.125 * jnp.einsum("rgd,cd->grc", query, keys, preferred_element_type=F32)
    scores = jnp.where(allowed[None], scores, MASKED)
    sink = attention_sink_logits.astype(F32)[:, None]
    peak = jnp.maximum(jnp.max(scores, axis=-1), sink)
    exp_scores = jnp.exp(scores - peak[..., None])
    sink_exp = jnp.exp(sink - peak)
    denom = jnp.sum(exp_scores, axis=-1) + sink_exp
    probs = exp_scores / denom[..., None]
    sink_prob = sink_exp / denom
    prob_low = probs.astype(BF)
    heads_out = (
        jnp.einsum("grc,cd->rgd", prob_low, values, preferred_element_type=F32)
        .astype(BF)
        .reshape(rows, q_cols)
    )
    heads_all = lax.all_gather(heads_out, "dp")
    out_full = out_all[:, :chunk].reshape(width, q_cols)

    branch = padded(dot(heads_out, out_full, ((1,), (1,))).astype(BF))
    branch = exchange(branch.reshape(rows, tn, cols).transpose(1, 0, 2), "tensor")
    branch = jnp.sum(branch.astype(F32), axis=0)
    hidden_cols = my_cols(padded(inputs + bias_out[None])) + branch
    gain_cols = lax.dynamic_slice_in_dim(jnp.pad(gain_two, (0, wide - width)), me_t * cols, cols, 0)
    out_rows = dot(place2, (hidden_cols * gain_cols[None]).astype(BF)).astype(BF)
    expert_cols = exchange(out_rows.reshape(experts, cap, cols), "dp").reshape(slots, cols)
    expert_in = lax.all_gather(expert_cols, "tensor")
    expert_in = expert_in.transpose(1, 0, 2).reshape(slots, wide)[:, :width]

    hidden_state = (
        spread(hidden_cols.astype(BF), "tensor")
        .transpose(1, 0, 2)
        .reshape(rows, wide)[:, :width]
        .astype(F32)
    )
    scale_two = lax.rsqrt(jnp.mean(hidden_state * hidden_state, axis=-1, keepdims=True) + EPSILON)
    normed_two = hidden_state * scale_two
    second_in = (normed_two * gain_two).astype(BF)
    bias_router = router_bias.astype(F32)

    def gates_of(logits, chosen):
        top = jnp.max(jnp.where(chosen > 0, logits, MASKED), axis=-1, keepdims=True)
        weights = jnp.where(chosen > 0, jnp.exp(logits - top), 0.0)
        total = jnp.sum(weights, axis=-1, keepdims=True)
        return weights / jnp.where(total > 0, total, 1.0)

    gates = gates_of(dot(second_in, router_t, ((1,), (1,))) + bias_router, member_f)

    w_gate, w_up, w_down = gate_weight[0], up_weight[0], down_weight[0]
    grads_in = grad_rows[:, :width]
    chosen = grad_rows[:, width : width + experts].astype(F32)
    down_back = dot(grads_in, w_down, ((1,), (1,)))
    square = jnp.square(expert_in.astype(F32) / gain_two[None])
    row_scale = lax.rsqrt(jnp.mean(square, axis=-1, keepdims=True) + EPSILON)
    row_gates = gates_of(
        row_scale * dot(expert_in, router_t, ((1,), (1,))) + bias_router, chosen
    )
    mine = (expert_ids == me_dp).astype(F32)
    gate_of_row = jnp.sum(row_gates * mine[None], axis=-1, keepdims=True)
    gate_in = row_scale * dot(expert_in, w_gate) + gate_bias[0].astype(F32)
    up_in = row_scale * dot(expert_in, w_up) + up_bias[0].astype(F32)
    gate_tanh = jnp.tanh(gate_in / 7.0)
    up_tanh = jnp.tanh(up_in / 7.0)
    gate_c = 7.0 * gate_tanh
    up_c = 7.0 * up_tanh
    sigma = jax.nn.sigmoid(1.702 * gate_c)
    glu = gate_c * sigma
    hidden = ((up_c + 1.0) * glu).astype(BF)
    bias_down = down_bias[0].astype(F32)
    bias_on = (me_t == 0).astype(F32)
    act_grad = gate_of_row * down_back
    gate_grad = (
        act_grad
        * (up_c + 1.0)
        * (sigma + 1.702 * gate_c * sigma * (1.0 - sigma))
        * (1.0 - gate_tanh * gate_tanh)
    ).astype(BF)
    up_grad = (act_grad * glu * (1.0 - up_tanh * up_tanh)).astype(BF)
    gates_part = jnp.sum(hidden.astype(F32) * down_back, axis=-1, keepdims=True) + bias_on * dot(
        grads_in, down_bias[0][:, None]
    )
    rows_back = dot(gate_grad, w_gate, ((1,), (1,))) + dot(up_grad, w_up, ((1,), (1,)))
    gates_high, gates_low = high_low(gates_part)
    rows_back = jnp.concatenate(
        [
            rows_back.astype(BF),
            gates_high,
            gates_low,
            jnp.zeros((slots, wide - width - 2), BF),
        ],
        axis=1,
    )

    def summed(value):
        got = exchange(value.reshape(slots, tn, cols).transpose(1, 0, 2), "tensor")
        return jnp.sum(got.astype(F32), axis=0)

    back_cols = summed(rows_back)
    gates_high, gates_low = high_low(back_cols[:, spare + 0 : spare + 1] + back_cols[:, spare + 1 : spare + 2])
    last = (me_t == tn - 1).astype(BF)
    back_low = back_cols.astype(BF)
    back_low = jnp.concatenate(
        [
            back_low[:, :spare],
            jnp.where(me_t == tn - 1, gates_high, back_low[:, spare : spare + 1]),
            jnp.where(me_t == tn - 1, gates_low, back_low[:, spare + 1 : spare + 2]),
            back_low[:, spare + 2 :],
        ],
        axis=1,
    )
    back_got = exchange(back_low.reshape(experts, cap, cols), "dp")
    back_tokens = dot(place2, back_got.reshape(slots, cols), ((0,), (0,))).astype(BF)
    gates_back = jnp.einsum(
        "ers,erk->ske", place, back_got[:, :, spare : spare + 2], preferred_element_type=F32
    ).astype(BF).reshape(rows, 2 * experts)
    back_tokens = jnp.where(
        me_t == tn - 1,
        jnp.concatenate(
            [
                back_tokens[:, :spare],
                gates_back,
                jnp.zeros((rows, cols - spare - 2 * experts), BF),
            ],
            axis=1,
        ),
        back_tokens,
    )
    back_all = spread(back_tokens, "tensor").transpose(1, 0, 2).reshape(rows, wide)
    gate_grads = back_all[:, width : width + experts].astype(F32) + back_all[
        :, width + experts : width + 2 * experts
    ].astype(F32)
    logit_grad = gates * (gate_grads - jnp.sum(gates * gate_grads, axis=-1, keepdims=True))
    second_grad = back_all[:, :width].astype(F32) + dot(logit_grad.astype(BF), router_t)
    grad_router = dot(logit_grad.astype(BF), second_in, ((0,), (0,)))
    grad_router_bias = jnp.sum(logit_grad, axis=0)

    grad_out = cotangent.astype(F32)
    scaled = second_grad * gain_two
    state_grad = grad_out + scale_two * (
        scaled - normed_two * jnp.mean(scaled * normed_two, axis=-1, keepdims=True)
    )
    grad_mlp_gain = jnp.sum(second_grad * normed_two, axis=0)
    state_low = state_grad.astype(BF)
    heads_grad = dot(state_low, out_full).astype(BF).reshape(rows, q_heads, hd)

    prob_grad = jnp.einsum("rgd,cd->grc", heads_grad, values, preferred_element_type=F32)
    row_delta = jnp.sum(probs * prob_grad, axis=-1)
    score_grad = (probs * (prob_grad - row_delta[..., None])).astype(BF)
    grad_sinks = -jnp.sum(sink_prob * row_delta, axis=-1)
    query_grad = 0.125 * jnp.einsum("grc,cd->rgd", score_grad, keys, preferred_element_type=F32)
    keys_grad = 0.125 * jnp.einsum("grc,rgd->cd", score_grad, query, preferred_element_type=F32)
    values_grad = jnp.einsum("grc,rgd->cd", prob_low, heads_grad, preferred_element_type=F32)
    kv_grad = jnp.concatenate([keys_grad, values_grad], axis=1)
    rim_grad = lax.ppermute(
        kv_grad[:window].astype(BF), "dp", [(i + 1, i) for i in range(dp - 1)]
    )
    kv_grad = kv_grad[window:] + rim_grad.astype(F32)
    lin_grad = jnp.concatenate(
        [
            rotate(query_grad, cos, -sin).reshape(rows, q_cols),
            rotate(kv_grad[:, None, :hd], cos, -sin)[:, 0],
            kv_grad[:, hd:],
        ],
        axis=1,
    ).astype(BF)

    sink_rows = jnp.pad(
        jnp.stack(high_low(grad_sinks)), ((0, 14), (0, qkv_cols - q_heads))
    )
    lin_all = lax.all_gather(jnp.concatenate([lin_grad, sink_rows], axis=0), "dp")
    half = rows // 2
    lin_first = lin_all[:, :half].reshape(dp * half, qkv_cols)
    lin_second = lin_all[:, half:rows].reshape(dp * half, qkv_cols)
    grad_qkv = dot(first_chunk[0], lin_first, ((0,), (0,))) + dot(
        first_chunk[1], lin_second, ((0,), (0,))
    )
    grad_bias = jnp.sum(lin_all[:, :rows].astype(F32), axis=(0, 1))
    grad_sinks = jnp.sum(lin_all[:, rows : rows + 2, :q_heads].astype(F32), axis=(0, 1))

    qkv_full = qkv_all[:, :chunk].reshape(width, qkv_cols)
    first_part = dot(lin_grad, qkv_full, ((1,), (1,))).astype(BF)
    own_rows = rows // tn
    first_rows = jnp.sum(
        exchange(first_part.reshape(tn, own_rows, width), "tensor").astype(F32), axis=0
    )

    def my_rows(a):
        return lax.dynamic_slice_in_dim(a, me_t * own_rows, own_rows, 0)

    normed_mine = my_rows(normed_one)
    scaled_one = first_rows * gain_one
    grad_rows_mine = my_rows(state_grad) + my_rows(scale_one) * (
        scaled_one - normed_mine * jnp.mean(scaled_one * normed_mine, axis=-1, keepdims=True)
    )
    gain_part = jnp.sum(own_qkv.astype(F32) * grad_qkv, axis=1)
    gain_rows = jnp.pad(jnp.stack(high_low(gain_part)), ((0, 14), (0, width - chunk)))
    input_all = spread(jnp.concatenate([grad_rows_mine.astype(BF), gain_rows], axis=0), "tensor")
    grad_input = input_all[:, :own_rows].reshape(rows, width).astype(F32)
    grad_attn_gain = jnp.sum(
        input_all[:, own_rows : own_rows + 2, :chunk].astype(F32), axis=(0, 1)
    ) / attn_gain.astype(F32)

    down_out = gate_of_row * (dot(hidden, w_down) + bias_on * bias_down)
    mixed_cols = summed(padded(down_out.astype(BF))).astype(BF).reshape(experts, cap, cols)
    vectors = jnp.concatenate([grad_router, grad_mlp_gain[None], jnp.zeros((1, width), F32)])
    vectors = jnp.pad(
        vectors.astype(BF).reshape(9, 2, dp, chunk), ((0, 0), (0, 0), (0, 0), (0, chunk_pad - chunk))
    )
    vectors = vectors.transpose(2, 0, 1, 3).reshape(dp, 9, 2 * chunk_pad)
    bias_row = jnp.pad(jnp.concatenate(high_low(grad_router_bias)), (0, cols - 2 * experts))
    bias_row = jnp.broadcast_to(bias_row[None, None], (dp, 1, cols))
    last_got = exchange(
        jnp.concatenate(
            [mixed_cols, by_chunk(state_low), vectors, bias_row, jnp.zeros((dp, 6, cols), BF)], axis=1
        ),
        "dp",
    )
    mixture = dot(place2, last_got[:, :cap].reshape(slots, cols), ((0,), (0,))).astype(BF)
    mixture = spread(mixture, "tensor").transpose(1, 0, 2).reshape(rows, wide)[:, :width]
    block_out = hidden_state + mixture.astype(F32)

    state_chunk = of_chunk(last_got[:, cap : cap + half])
    heads_first = heads_all[:, :half].reshape(dp * half, q_cols)
    heads_second = heads_all[:, half:].reshape(dp * half, q_cols)
    grad_out_weight = dot(state_chunk[0], heads_first, ((0,), (0,))) + dot(
        state_chunk[1], heads_second, ((0,), (0,))
    )
    grad_out_bias = jnp.sum(state_chunk[0].astype(F32), axis=0) + jnp.sum(
        state_chunk[1].astype(F32), axis=0
    )
    sums = jnp.sum(last_got[:, cap + half :].astype(F32), axis=0)
    vectors = sums[:9].reshape(18, chunk_pad)[:, :chunk]
    grad_router_weight = vectors[:experts].T
    grad_mlp_gain = vectors[experts]
    grad_router_bias = sums[9, :experts] + sums[9, experts : 2 * experts]

    low_gate = (row_scale * gate_grad.astype(F32)).astype(BF)
    low_up = (row_scale * up_grad.astype(F32)).astype(BF)
    grad_gate_weight = dot(expert_in, low_gate, ((0,), (0,)))
    grad_up_weight = dot(expert_in, low_up, ((0,), (0,)))
    grad_gate_bias = jnp.sum(gate_grad.astype(F32), axis=0)
    grad_up_bias = jnp.sum(up_grad.astype(F32), axis=0)
    low_hidden = (gate_of_row * hidden.astype(F32)).astype(BF)
    grad_down_weight = dot(low_hidden, grads_in, ((0,), (0,)))
    gate_rows = jnp.concatenate(high_low(gate_of_row), axis=1)
    grad_down_bias = jnp.sum(dot(gate_rows, grads_in, ((0,), (0,))), axis=0)

    return (
        block_out,
        grad_input,
        grad_attn_gain,
        grad_qkv[:, :q_cols],
        grad_bias[:q_cols],
        grad_qkv[:, q_cols : q_cols + hd],
        grad_bias[q_cols : q_cols + hd],
        grad_qkv[:, q_cols + hd :],
        grad_bias[q_cols + hd :],
        grad_sinks,
        grad_out_weight,
        grad_out_bias,
        grad_mlp_gain,
        grad_router_weight,
        grad_router_bias,
        grad_gate_weight[None],
        grad_gate_bias[None],
        grad_up_weight[None],
        grad_up_bias[None],
        grad_down_weight[None],
        grad_down_bias[None],
    )


def solution(mesh):
    return jax.shard_map(
        local,
        mesh=mesh,
        in_specs=(
            P("dp", None),
            P("dp"),
            P("dp", "tensor"),
            P("tensor"),
            P("dp", "tensor"),
            P("tensor"),
            P("dp", "tensor"),
            P("tensor"),
            P("tensor"),
            P("dp", "tensor"),
            P("dp"),
            P("dp"),
            P("dp", None),
            P(),
            P("dp", None, "tensor"),
            P("dp", "tensor"),
            P("dp", None, "tensor"),
            P("dp", "tensor"),
            P("dp", "tensor", None),
            P("dp", None),
            P("dp", None),
            P(),
            P("dp", None),
        ),
        out_specs=(
            P("dp", None),
            P("dp", None),
            P("dp"),
            P("dp", "tensor"),
            P("tensor"),
            P("dp", "tensor"),
            P("tensor"),
            P("dp", "tensor"),
            P("tensor"),
            P("tensor"),
            P("dp", "tensor"),
            P("dp"),
            P("dp"),
            P("dp", None),
            P(),
            P("dp", None, "tensor"),
            P("dp", "tensor"),
            P("dp", None, "tensor"),
            P("dp", "tensor"),
            P("dp", "tensor", None),
            P("dp", None),
        ),
        check_vma=False,
    )
```

time: 1340 us -> 824 us (0.61)
  blocking collectives: 494 us -> 94.8 us
  waiting for transfers between devices: 489 us -> 324 us
  starting transfers between devices: 44.2 us -> 96.3 us
  other arithmetic: 67.2 us -> 49.8 us
    unnamed x3 -> x0, blocking collectives: 214 us -> none
    psum x3 -> x0, waiting for transfers between devices: 208 us -> none  [the longest x1 77 us: local(): lax.psum(combined.astype(jnp.bfloat16), 'tensor').astype(jnp.float32)]
    all_gather x3 -> x0, blocking collectives: 154 us -> none  [the longest x1 108 us: local(): lax.all_gather(router_weight, 'dp', axis=0, tiled=True)]
    all_gather x2 -> x6, waiting for transfers between devices: 0.02 us -> 141 us  [the longest x1 48.6 us: local(): qkv_all = lax.all_gather(jnp.concatenate([own_qkv, extras], axis=0), 'dp')]
    all_to_all x3 -> x10, waiting for transfers between devices: 254 us -> 182 us  [exchange(): return lax.all_to_all(value, axis, split_axis=0, concat_axis=0, tiled=True)]
    all_to_all x3 -> x10, starting transfers between devices: 24 us -> 92.1 us  [exchange(): return lax.all_to_all(value, axis, split_axis=0, concat_axis=0, tiled=True)]
    gather x7 -> x0, local copies, waits for them, and re-layouts: 64.3 us -> none  [the longest x2 19 us: local(): returned[slot_pos]]
    psum x2 -> x0, blocking collectives: 50.9 us -> none  [the longest x1 33.8 us: local(): lax.psum((grad_query_bias, grad_key_bias, grad_value_bias, grad_sinks, gr...]
  transfers between devices with their start and end apart: 15 -> 18, of which waited for: 6 -> 13; matrix products, arithmetic and copies ran while one was open for 15% -> 21% of each run, Pallas kernels for 0% -> 0%
where the time goes in v1:
time: 824 us; the launch traced here: 811 us
  waiting for transfers between devices  324 us (39%)
  local copies, waits for them, and re-layouts  141 us (17%)
  starting transfers between devices  96.3 us (12%)
  blocking collectives  94.8 us (12%)
  matrix products  88.9 us (11%)
  other arithmetic  49.8 us (6%)
  between operations  16.3 us (2%)
    all_to_all x10, waiting for transfers between devices, exchange(): return lax.all_to_all(value, axis, split_axis=0, concat_axis=0, tiled=True)  182 us
    all_to_all x2, blocking collectives, exchange(): return lax.all_to_all(value, axis, split_axis=0, concat_axis=0, tiled=True)  94.8 us
    all_to_all x10, starting transfers between devices, exchange(): return lax.all_to_all(value, axis, split_axis=0, concat_axis=0, tiled=True)  92.1 us
    dot_general x28, matrix products, dot(): return lax.dot_general(a, b, (dims, ((), ())), preferred_element_type=F32)  86.7 us
    all_gather x1, waiting for transfers between devices, local(): qkv_all = lax.all_gather(jnp.concatenate([own_qkv, extras], axis=0), 'dp')  48.6 us
    all_gather x1, waiting for transfers between devices, local(): lax.all_gather(jnp.pad(out_weight, ((0, chunk_pad - chunk), (0, 0))), 'dp')  47.2 us
    all_gather x1, waiting for transfers between devices, local(): lax.all_gather(first_got[:, :cap].reshape(slots, cols), 'tensor')  45.2 us
    concatenate x1, local copies, waits for them, and re-layouts, local(): jnp.concatenate([rows_back.astype(BF), gates_high, gates_low, jnp.zeros((...  28.1 us
  transfers between devices with their start and end apart: 18, of which 13 were waited for; matrix products, arithmetic and copies ran while one was open for 21% of the time, Pallas kernels for 0%

profile of v1, /device:TPU:0, one launch (start us, length us, event | category | flops | bytes accessed | tf_op | source)
XLA Modules:
  0.0 810.8 jit_solution(10068349624985604703)
XLA Ops:
  18.7 47.2 %all-gather.18.cloned.1.call-done = bf16[3072,512]{1,0:T(8,128)(2,1)} async-done(((bf16[192,512]{1,0:T(8,128)(2,1)}), bf16[3072,512]{1,0:T(8,128)(2,1)}) %all-gather.18.cloned.1.call-update) | async-done | bytes 3145744 | tf_op jit(solution)/shard_map/all_gather | solution.py:133
  74.0 48.6 %all-gather.16.cloned.1.call-done = bf16[3072,640]{1,0:T(8,128)(2,1)} async-done(((bf16[192,640]{1,0:T(8,128)(2,1)}), bf16[3072,640]{1,0:T(8,128)(2,1)}) %all-gather.16.cloned.1.call-update) | async-done | bytes 3932176 | tf_op jit(solution)/shard_map/all_gather | solution.py:132
  152.5 12.9 %all-to-all-done = bf16[8,128,384]{1,2,0:T(8,128)(2,1)} async-done(((bf16[8,128,384]{1,2,0:T(8,128)(2,1)}), bf16[8,128,384]{1,2,0:T(8,128)(2,1)}, u32[]{:S(2)}, u32[]{:S(2)}) %all-to-all-start) | async-done | bytes 786464 | tf_op jit(solution)/shard_map/all_to_all | solution.py:39
  169.7 21.8 %all_to_all.60 = bf16[16,64,384]{2,1,0:T(8,128)(2,1)} all-to-all(bf16[16,64,384]{2,1,0:T(8,128)(2,1)S(1)} %bitcast.237), channel_id=1, replica_groups=mesh['dp'=16,'tensor'=8] {'dp'}, dimensions={0} | all-to-all | bytes 1572864 | tf_op jit(solution)/shard_map/all_to_all | solution.py:39
  203.6 73.0 %all_to_all.61 = bf16[16,128,384]{2,1,0:T(8,128)(2,1)S(1)} all-to-all(bf16[16,128,384]{2,1,0:T(8,128)(2,1)S(1)} %maximum_maximum_fusion), channel_id=1, replica_groups=mesh['dp'=16,'tensor'=8] {'dp'}, dimensions={0} | all-to-all | bytes 3145728 | tf_op jit(solution)/shard_map/all_to_all | solution.py:39
  283.0 8.7 %copy.285 = bf16[8,1024,384]{1,2,0:T(8,128)(2,1)} copy(bf16[8,1024,384]{2,1,0:T(8,128)(2,1)} %all-gather.12.cloned.1.call-done) | data formatting | bytes 12582912 | tf_op jit(solution)/shard_map/all_gather | solution.py:217
  296.6 6.3 multiply_tanh_fusion
  303.0 45.2 %all-gather.10.cloned.1.call-done = bf16[8,1024,384]{2,1,0:T(8,128)(2,1)} async-done(((bf16[1,1024,384]{2,1,0:T(8,128)(2,1)}), bf16[8,1024,384]{2,1,0:T(8,128)(2,1)}) %all-gather.10.cloned.1.call-update) | async-done | bytes 6291472 | tf_op jit(solution)/shard_map/all_gather | solution.py:157
  348.1 8.7 %copy.284 = bf16[1024,8,384]{0,2,1:T(8,128)(2,1)} copy(bf16[1024,8,384]{2,0,1:T(8,128)(2,1)} %bitcast.231) | data formatting | bytes 12582912 | tf_op jit(solution)/shard_map/transpose | solution.py:158
  361.9 5.9 fusion.5
  382.9 28.1 %concatenate.110 = bf16[1024,3072]{0,1:T(8,128)(2,1)} concatenate(bf16[1024,2880]{0,1:T(8,128)(2,1)} %add_convert_fusion, bf16[1024,1]{0,1:T(2,128)(2,1)S(1)} %convert_element_type.510, bf16[1024,1]{0,1:T(2,128)(2,1)S(1)} %convert_element_type.513, bf16[1024,190]{0,1:T(8,128)(2,1)S(1)} %broadcast_in_dim.102), dimensions={1} | concatenate | bytes 12582912 | tf_op jit(solution)/shard_map/concatenate | solution.py:274
  416.0 72.1 %all-to-all-done.5 = bf16[8,1024,384]{1,2,0:T(8,128)(2,1)} async-done(((bf16[8,1024,384]{1,2,0:T(8,128)(2,1)}), bf16[8,1024,384]{1,2,0:T(8,128)(2,1)}, u32[]{:S(2)}, u32[]{:S(2)}) %all-to-all-start.5) | async-done | bytes 6291488 | tf_op jit(solution)/shard_map/all_to_all | solution.py:39
  489.1 26.4 %all-to-all-start.1 = ((bf16[8,128,384]{2,1,0:T(8,128)(2,1)}), bf16[8,128,384]{2,1,0:T(8,128)(2,1)}, u32[]{:S(2)}, u32[]{:S(2)}) async-start(bf16[8,128,384]{2,1,0:T(8,128)(2,1)} %broadcast_in_dim.98), calls=%async_computation.1 | async-start | bytes 1572864 | tf_op jit(solution)/shard_map/all_to_all | solution.py:39
  521.5 6.1 all-to-all-done.1
  527.6 6.7 all-to-all-start.6
  542.6 6.9 all-to-all-done.6
  570.8 7.3 convolution_bitcast_fusion.1
  579.1 48.0 %all-to-all-done.4 = bf16[8,1024,384]{1,2,0:T(8,128)(2,1)} async-done(((bf16[8,1024,384]{1,2,0:T(8,128)(2,1)}), bf16[8,1024,384]{1,2,0:T(8,128)(2,1)}, u32[]{:S(2)}, u32[]{:S(2)}) %all-to-all-start.4) | async-done | bytes 6291488 | tf_op jit(solution)/shard_map/all_to_all | solution.py:39
  628.0 25.9 %all-to-all-start.7 = ((bf16[8,128,384]{2,1,0:T(8,128)(2,1)}), bf16[8,128,384]{2,1,0:T(8,128)(2,1)}, u32[]{:S(2)}, u32[]{:S(2)}) async-start(bf16[8,128,384]{2,1,0:T(8,128)(2,1)} %broadcast_in_dim.104), calls=%async_computation.7 | async-start | bytes 1572864 | tf_op jit(solution)/shard_map/all_to_all | solution.py:39
  660.3 7.2 convolution_bitcast_fusion.2
  701.0 6.8 concatenate.116
  718.4 7.2 convolution_bitcast_fusion
  729.1 17.5 %all-to-all-done.8 = bf16[16,144,384]{2,1,0:T(8,128)(2,1)} async-done(((bf16[16,144,384]{2,1,0:T(8,128)(2,1)}), bf16[16,144,384]{2,1,0:T(8,128)(2,1)}, u32[]{:S(2)}, u32[]{:S(2)}) %all-to-all-start.8) | async-done | bytes 1769504 | tf_op jit(solution)/shard_map/all_to_all | solution.py:39
  787.3 9.5 %all-to-all-done.11 = bf16[8,32,2880]{2,1,0:T(8,128)(2,1)} async-done(((bf16[8,32,2880]{2,1,0:T(8,128)(2,1)}), bf16[8,32,2880]{2,1,0:T(8,128)(2,1)}, u32[]{:S(2)}, u32[]{:S(2)}) %all-to-all-start.11) | async-done | bytes 1474592 | tf_op jit(solution)/shard_map/all_to_all | solution.py:39
  (436 shorter events, 240.5 us)
Async XLA Ops:
  7.2 360.7 %copy-start = (bf16[1,2880,360]{1,2,0:T(8,128)(2,1)S(1)}, bf16[1,2880,360]{1,2,0:T(8,128)(2,1)}, u32[]{:S(2)}) copy-start(bf16[1,2880,360]{1,2,0:T(8,128)(2,1)} %param.39) | copy-start | bytes 6220804
  7.3 58.6 %all-gather.18.cloned.1.call-start = ((), (), s32[]{:S(2)}) async-start(), calls=%async_computation.16 | async-start | bytes 3342336 | tf_op jit(solution)/shard_map/all_gather | solution.py:133
  9.1 113.5 %all-gather.16.cloned.1.call-start = ((), (), s32[]{:S(2)}) async-start(), calls=%async_computation.15 | async-start | bytes 4177920 | tf_op jit(solution)/shard_map/all_gather | solution.py:132
  17.1 125.7 %copy-start.55 = (f32[8]{0:T(128)}, f32[8]{0:T(128)S(1)}, u32[]{:S(2)}) copy-start(f32[8]{0:T(128)S(1)} %convert_element_type.480) | copy-start | bytes 100
  17.3 121.6 %copy-start.51 = (f32[32]{0:T(128)}, f32[32]{0:T(128)S(1)}, u32[]{:S(2)}) copy-start(f32[32]{0:T(128)S(1)} %multiply_power_fusion) | copy-start | bytes 388
  17.8 121.2 %copy-start.53 = (f32[128]{0:T(128)}, f32[128]{0:T(128)S(1)}, u32[]{:S(2)}) copy-start(f32[128]{0:T(128)S(1)} %subtract_convert_fusion.6) | copy-start | bytes 1540
  139.2 3.0 collective-permute-start
  146.6 18.7 %all-to-all-start = ((bf16[8,128,384]{1,2,0:T(8,128)(2,1)}), bf16[8,128,384]{1,2,0:T(8,128)(2,1)}, u32[]{:S(2)}, u32[]{:S(2)}) async-start(bf16[8,128,384]{1,2,0:T(8,128)(2,1)} %bitcast.236), calls=%async_computation | async-start | bytes 1572864 | tf_op jit(solution)/shard_map/all_to_all | solution.py:39
  151.0 131.9 %all-gather.12.cloned.1.call-start = ((), (), s32[]{:S(2)}) async-start(), calls=%async_computation.13 | async-start | bytes 7077888 | tf_op jit(solution)/shard_map/all_gather | solution.py:217
  191.5 156.6 %all-gather.10.cloned.1.call-start = ((), (), s32[]{:S(2)}) async-start(), calls=%async_computation.12 | async-start | bytes 7077888 | tf_op jit(solution)/shard_map/all_gather | solution.py:157
  411.0 77.1 %all-to-all-start.5 = ((bf16[8,1024,384]{1,2,0:T(8,128)(2,1)}), bf16[8,1024,384]{1,2,0:T(8,128)(2,1)}, u32[]{:S(2)}, u32[]{:S(2)}) async-start(bf16[8,1024,384]{1,2,0:T(8,128)(2,1)} %bitcast.203), calls=%async_computation.5 | async-start | bytes 12582912 | tf_op jit(solution)/shard_map/all_to_all | solution.py:39
  489.1 38.5 %all-to-all-start.1 = ((bf16[8,128,384]{2,1,0:T(8,128)(2,1)}), bf16[8,128,384]{2,1,0:T(8,128)(2,1)}, u32[]{:S(2)}, u32[]{:S(2)}) async-start(bf16[8,128,384]{2,1,0:T(8,128)(2,1)} %broadcast_in_dim.98), calls=%async_computation.1 | async-start | bytes 1572864 | tf_op jit(solution)/shard_map/all_to_all | solution.py:39
  527.6 21.9 %all-to-all-start.6 = ((bf16[16,64,384]{2,1,0:T(8,128)(2,1)}), bf16[16,64,384]{2,1,0:T(8,128)(2,1)S(1)}, u32[]{:S(2)}, u32[]{:S(2)}) async-start(bf16[16,64,384]{2,1,0:T(8,128)(2,1)} %bitcast.40), calls=%async_computation.6 | async-start | bytes 1572864 | tf_op jit(solution)/shard_map/all_to_all | solution.py:39
  550.4 76.7 %all-to-all-start.4 = ((bf16[8,1024,384]{1,2,0:T(8,128)(2,1)}), bf16[8,1024,384]{1,2,0:T(8,128)(2,1)}, u32[]{:S(2)}, u32[]{:S(2)}) async-start(bf16[8,1024,384]{1,2,0:T(8,128)(2,1)} %bitcast.202), calls=%async_computation.4 | async-start | bytes 12582912 | tf_op jit(solution)/shard_map/all_to_all | solution.py:39
  555.3 202.8 %all-gather.14.cloned.1.call-start = ((), (), s32[]{:S(2)}) async-start(), calls=%async_computation.14 | async-start | bytes 2228224 | tf_op jit(solution)/shard_map/all_gather | solution.py:207
  570.0 105.9 %copy-start.67 = (f32[128]{0:T(128)}, f32[128]{0:T(128)S(1)}, u32[]{:S(2)}) copy-start(f32[128]{0:T(128)S(1)} %add_rsqrt_fusion.1) | copy-start | bytes 1540
  628.0 45.0 %all-to-all-start.7 = ((bf16[8,128,384]{2,1,0:T(8,128)(2,1)}), bf16[8,128,384]{2,1,0:T(8,128)(2,1)}, u32[]{:S(2)}, u32[]{:S(2)}) async-start(bf16[8,128,384]{2,1,0:T(8,128)(2,1)} %broadcast_in_dim.104), calls=%async_computation.7 | async-start | bytes 1572864 | tf_op jit(solution)/shard_map/all_to_all | solution.py:39
  653.9 112.2 %all-gather.20.cloned.1.call-start = ((), (), s32[]{:S(2)}) async-start(), calls=%async_computation.17 | async-start | bytes 3133440 | tf_op jit(solution)/shard_map/all_gather | solution.py:360
  681.3 5.4 collective-permute-start.1
  694.0 19.5 %all-to-all-start.10 = ((bf16[8,16,2880]{2,1,0:T(8,128)(2,1)}), bf16[8,16,2880]{2,1,0:T(8,128)(2,1)}, u32[]{:S(2)}, u32[]{:S(2)}) async-start(bf16[8,16,2880]{2,1,0:T(8,128)(2,1)} %bitcast.57), calls=%async_computation.10 | async-start | bytes 1507328 | tf_op jit(solution)/shard_map/all_to_all | solution.py:39
  713.5 33.1 %all-to-all-start.8 = ((bf16[16,144,384]{2,1,0:T(8,128)(2,1)}), bf16[16,144,384]{2,1,0:T(8,128)(2,1)}, u32[]{:S(2)}, u32[]{:S(2)}) async-start(bf16[16,144,384]{2,1,0:T(8,128)(2,1)} %concatenate.116), calls=%async_computation.8 | async-start | bytes 3538944 | tf_op jit(solution)/shard_map/all_to_all | solution.py:39
  725.7 21.0 %copy-start.50 = (s32[16,128]{1,0:T(8,128)S(1)}, s32[16,128]{1,0:T(8,128)}, u32[]{:S(2)}) copy-start(s32[16,128]{1,0:T(8,128)} %copy-done.48) | copy-start | bytes 24580
  749.1 16.8 %all-to-all-start.9 = ((bf16[8,128,384]{2,1,0:T(8,128)(2,1)}), bf16[8,128,384]{2,1,0:T(8,128)(2,1)S(1)}, u32[]{:S(2)}, u32[]{:S(2)}) async-start(bf16[8,128,384]{2,1,0:T(8,128)(2,1)} %broadcast_in_dim.111), calls=%async_computation.9 | async-start | bytes 1572864 | tf_op jit(solution)/shard_map/all_to_all | solution.py:39
  771.7 25.0 %all-to-all-start.11 = ((bf16[8,32,2880]{2,1,0:T(8,128)(2,1)}), bf16[8,32,2880]{2,1,0:T(8,128)(2,1)}, u32[]{:S(2)}, u32[]{:S(2)}) async-start(bf16[8,32,2880]{2,1,0:T(8,128)(2,1)} %broadcast_in_dim.113), calls=%async_computation.11 | async-start | bytes 3014656 | tf_op jit(solution)/shard_map/all_to_all | solution.py:39
  (83 other events, 366.6 us)
Sparse Core Ops, SparseCore 0:
  11.1 54.7 all-gather.17
  68.8 53.7 all-gather.15
  191.6 79.9 all-gather.11
  279.0 69.1 all-gather.9
  568.5 89.9 all-gather.13
  688.0 71.2 all-gather.19
